TPU v7x, 32 devices: a whole 2x2x4 slice. The times are simulated.
32 devices in a mesh: ctx: 8 (over z, y), head: 4 (over x, core).
Axes of the slice: x: 2, y: 2, z: 4, core: 2. Of those that a mesh axis runs over, the one named last changes fastest.
Arguments:
- queries: bfloat16 [3072, 1024], P('ctx', 'head'), may hold values from -6 to 6
- keys: bfloat16 [3072, 1024], P('ctx', 'head'), may hold values from -6 to 6
- values: bfloat16 [3072, 1024], P('ctx', 'head'), may hold values from -6 to 6
- out_weight: bfloat16 [1024, 5120], P('head'), may hold values from -1.1953125 to 1.1953125
- neighbours: int32 [8, 7], P('ctx'), may hold values from -1 to 7, as said below
- counts: int32 [8], P('ctx'), may hold values from 1 to 7
Outputs:
- projected: bfloat16 [3072, 5120], P(('ctx', 'head'))
Inputs may be any that keep to these rules, and one draw needn't show every extreme that they name: `neighbours`: for query tile g the first counts[g] entries are distinct tiles within 3 of g, g itself among them; the other entries are -1. Some tile lists 7 tiles.
All inputs are finite; a program needn't handle non-finite values.
Results may differ from a plain program's by a relative error of at most 0.019.
Values may be sent and summed in bfloat16 or wider, within the bound.
No kernel may reach another device: no remote copies, remote signals or barrier semaphores. Data moves between devices by JAX's collectives and lax.ppermute only.
A program may use at most 64 MiB of HBM per device.

v0:
```python
import math

import jax
import jax.numpy as jnp
from jax import lax
from jax.sharding import PartitionSpec as P

HD = 128
REACH = 3


def passed_along(value, axis, steps):
    count = lax.axis_size(axis)
    first, last = (max(0, -steps), min(count, count - steps))
    return lax.ppermute(value, axis, [(source, source + steps) for source in range(first, last)])


def local(queries, keys, values, out_weight, neighbours, counts):
    row_count, feat_width = queries.shape
    tiles_dev = counts.shape[0]
    tile_rows = row_count // tiles_dev
    reach_dev = (REACH + tiles_dev - 1) // tiles_dev
    window_tiles = 2 * REACH + 1
    ctx_total = lax.axis_size("ctx")
    ctx_index = lax.axis_index("ctx")
    lower_keys = []
    lower_values = []
    upper_keys = []
    upper_values = []
    for distance in range(1, reach_dev + 1):
        from_below = passed_along((keys, values), "ctx", distance)
        from_above = passed_along((keys, values), "ctx", -distance)
        lower_keys.insert(0, from_below[0])
        lower_values.insert(0, from_below[1])
        upper_keys.append(from_above[0])
        upper_values.append(from_above[1])
    key_window = jnp.concatenate(lower_keys + [keys] + upper_keys, axis=0)
    value_window = jnp.concatenate(lower_values + [values] + upper_values, axis=0)
    heads_dev = feat_width // HD
    tile_total = tiles_dev * ctx_total
    offsets = jnp.arange(window_tiles, dtype=jnp.int32) - REACH
    slot_index = jnp.arange(window_tiles, dtype=jnp.int32)
    scale = 1.0 / math.sqrt(HD)

    def one_tile(local_tile):
        tile_index = ctx_index * tiles_dev + local_tile
        target = tile_index + offsets
        listing = lax.dynamic_index_in_dim(neighbours, local_tile, 0, keepdims=False)
        slot_count = lax.dynamic_index_in_dim(counts, local_tile, 0, keepdims=False)
        member = jnp.any(
            (listing[None, :] == target[:, None]) & (slot_index[None, :] < slot_count), axis=1
        )
        allowed = member & (target >= 0) & (target < tile_total)
        key_mask = jnp.repeat(allowed, tile_rows)

        def one_head(head_index):
            q_head = lax.dynamic_slice_in_dim(queries, head_index * HD, HD, 1)
            k_head = lax.dynamic_slice_in_dim(key_window, head_index * HD, HD, 1)
            v_head = lax.dynamic_slice_in_dim(value_window, head_index * HD, HD, 1)
            scores = (
                jnp.einsum("qd,kd->qk", q_head, k_head, preferred_element_type=jnp.float32) * scale
            )
            scores = jnp.where(key_mask[None, :], scores, -1e30)
            row_max = jnp.max(scores, axis=1, keepdims=True)
            weights = jnp.where(key_mask[None, :], jnp.exp(scores - row_max), 0.0)
            weight_sum = jnp.sum(weights, axis=1, keepdims=True)
            weights_low = weights.astype(jnp.bfloat16)
            mixed = jnp.dot(weights_low, v_head, preferred_element_type=jnp.float32) / weight_sum
            return mixed.astype(jnp.bfloat16)

        per_head = lax.map(one_head, jnp.arange(heads_dev, dtype=jnp.int32))
        return jnp.transpose(per_head, (1, 0, 2)).reshape(tile_rows, feat_width)

    attended = lax.map(one_tile, jnp.arange(tiles_dev, dtype=jnp.int32)).reshape(
        row_count, feat_width
    )
    return lax.psum_scatter(
        jnp.dot(attended, out_weight, preferred_element_type=jnp.float32).astype(jnp.bfloat16),
        "head",
        scatter_dimension=0,
        tiled=True,
    )


def solution(mesh):
    placed = (
        P("ctx", "head"),
        P("ctx", "head"),
        P("ctx", "head"),
        P("head", None),
        P("ctx", None),
        P("ctx"),
    )
    return jax.shard_map(
        local, mesh=mesh, in_specs=placed, out_specs=P(("ctx", "head"), None), check_vma=False
    )
```

profile of v0, /device:TPU:0, one launch (start us, length us, event | category | flops | bytes accessed | tf_op | source)
XLA Modules:
  0.0 132.1 jit_solution(12971544497554697546)
XLA Ops:
  6.5 0.0 copy-start
  6.5 0.0 copy-start.3
  6.5 0.0 reduce-scatter.2.cloned.1.call-start
  6.5 6.8 %collective-permute-start = (bf16[384,256]{1,0:T(8,128)(2,1)}, bf16[384,256]{1,0:T(8,128)(2,1)}, u32[]{:S(2)}, u32[]{:S(2)}) collective-permute-start(bf16[384,256]{1,0:T(8,128)(2,1)} %param.9), channel_id=1, source_target_pairs={{0,12},{4,16},{8,20},{12,24},{16,28},{1,13},{5,17},{9,21},{13,25},... | collective-permute-start | bytes 589832 | tf_op jit(solution)/shard_map/ppermute | solution.py:15
  13.4 4.1 %collective-permute-start.1 = (bf16[384,256]{1,0:T(8,128)(2,1)}, bf16[384,256]{1,0:T(8,128)(2,1)}, u32[]{:S(2)}, u32[]{:S(2)}) collective-permute-start(bf16[384,256]{1,0:T(8,128)(2,1)} %param.9), channel_id=1, source_target_pairs={{0,8},{4,12},{8,16},{12,20},{16,24},{20,28},{1,9},{5,13},{9,17},{1... | collective-permute-start | bytes 589832 | tf_op jit(solution)/shard_map/ppermute | solution.py:15
  17.5 2.8 %collective-permute-start.2 = (bf16[384,256]{1,0:T(8,128)(2,1)}, bf16[384,256]{1,0:T(8,128)(2,1)S(1)}, u32[]{:S(2)}, u32[]{:S(2)}) collective-permute-start(bf16[384,256]{1,0:T(8,128)(2,1)} %param.9), channel_id=1, source_target_pairs={{0,4},{4,8},{8,12},{12,16},{16,20},{20,24},{24,28},{1,5},{5,9},{9,... | collective-permute-start | bytes 589832 | tf_op jit(solution)/shard_map/ppermute | solution.py:15
  20.3 1.3 collective-permute-start.3
  21.6 1.3 collective-permute-start.4
  23.6 0.8 and_reduce_fusion
  24.4 0.0 collective-permute-done
  24.4 1.3 collective-permute-start.5
  25.7 0.9 constant_dynamic-update-slice_fusion.7
  26.7 0.0 collective-permute-done.1
  26.7 7.3 %collective-permute-start.6 = (bf16[384,256]{1,0:T(8,128)(2,1)}, bf16[384,256]{1,0:T(8,128)(2,1)S(1)}, u32[]{:S(2)}, u32[]{:S(2)}) collective-permute-start(bf16[384,256]{1,0:T(8,128)(2,1)} %param.10), channel_id=1, source_target_pairs={{0,12},{4,16},{8,20},{12,24},{16,28},{1,13},{5,17},{9,21},{13,25},... | collective-permute-start | bytes 589832 | tf_op jit(solution)/shard_map/ppermute | solution.py:15
  34.0 0.9 constant_dynamic-update-slice_fusion.6
  34.9 0.0 collective-permute-done.2
  34.9 3.7 %collective-permute-start.7 = (bf16[384,256]{1,0:T(8,128)(2,1)}, bf16[384,256]{1,0:T(8,128)(2,1)S(1)}, u32[]{:S(2)}, u32[]{:S(2)}) collective-permute-start(bf16[384,256]{1,0:T(8,128)(2,1)} %param.10), channel_id=1, source_target_pairs={{0,8},{4,12},{8,16},{12,20},{16,24},{20,28},{1,9},{5,13},{9,17},{1... | collective-permute-start | bytes 589832 | tf_op jit(solution)/shard_map/ppermute | solution.py:15
  38.6 0.9 constant_dynamic-update-slice_fusion.4
  39.6 0.7 collective-permute-done.6
  40.3 0.0 copy-done.3
  40.3 3.9 %collective-permute-start.8 = (bf16[384,256]{1,0:T(8,128)(2,1)S(1)}, bf16[384,256]{1,0:T(8,128)(2,1)S(1)}, u32[]{:S(2)}, u32[]{:S(2)}) collective-permute-start(bf16[384,256]{1,0:T(8,128)(2,1)S(1)} %copy-done.3), channel_id=1, source_target_pairs={{0,4},{4,8},{8,12},{12,16},{16,20},{20,24},{24,28},{1,5},{5,9},{9,... | collective-permute-start | bytes 589832 | tf_op jit(solution)/shard_map/ppermute | solution.py:15
  44.2 0.0 collective-permute-done.7
  44.2 1.3 collective-permute-start.9
  45.5 3.9 %collective-permute-done.8 = bf16[384,256]{1,0:T(8,128)(2,1)S(1)} collective-permute-done((bf16[384,256]{1,0:T(8,128)(2,1)S(1)}, bf16[384,256]{1,0:T(8,128)(2,1)S(1)}, u32[]{:S(2)}, u32[]{:S(2)}) %collective-permute-start.8) | collective-permute-done | bytes 196640 | tf_op jit(solution)/shard_map/ppermute | solution.py:15
  49.4 1.3 collective-permute-start.10
  50.7 0.0 copy-start.2
  50.8 0.0 collective-permute-done.3
  50.8 1.4 %collective-permute-start.11 = (bf16[384,256]{1,0:T(8,128)(2,1)S(1)}, bf16[384,256]{1,0:T(8,128)(2,1)S(1)}, u32[]{:S(2)}, u32[]{:S(2)}) collective-permute-start(bf16[384,256]{1,0:T(8,128)(2,1)S(1)} %copy-done.3), channel_id=1, source_target_pairs={{12,0},{16,4},{20,8},{24,12},{28,16},{13,1},{17,5},{21,9},{25,13},... | collective-permute-start | bytes 589832 | tf_op jit(solution)/shard_map/ppermute | solution.py:15
  52.2 0.9 constant_dynamic-update-slice_fusion.3
  53.2 0.0 collective-permute-done.4
  53.2 0.0 collective-permute-done.5
  53.2 0.0 copy-start.1
  53.2 0.0 collective-permute-done.9
  53.3 4.5 %collective-permute-done.10 = bf16[384,256]{1,0:T(8,128)(2,1)S(1)} collective-permute-done((bf16[384,256]{1,0:T(8,128)(2,1)S(1)}, bf16[384,256]{1,0:T(8,128)(2,1)S(1)}, u32[]{:S(2)}, u32[]{:S(2)}) %collective-permute-start.10) | collective-permute-done | bytes 196640 | tf_op jit(solution)/shard_map/ppermute | solution.py:15
  57.8 4.7 %collective-permute-done.11 = bf16[384,256]{1,0:T(8,128)(2,1)S(1)} collective-permute-done((bf16[384,256]{1,0:T(8,128)(2,1)S(1)}, bf16[384,256]{1,0:T(8,128)(2,1)S(1)}, u32[]{:S(2)}, u32[]{:S(2)}) %collective-permute-start.11) | collective-permute-done | bytes 196640 | tf_op jit(solution)/shard_map/ppermute | solution.py:15
  62.6 0.0 copy-start.4
  62.6 0.0 copy-done.1
  62.6 1.1 copy-done.4
  63.6 0.0 copy-done.2
  63.7 11.1 %while.18 = (s32[]{:T(128)}, bf16[2,384,128]{1,2,0:T(8,128)(2,1)S(1)}, s32[2]{0:T(128)S(1)}, bf16[384,256]{1,0:T(8,128)(2,1)S(1)}, bf16[2688,256]{1,0:T(8,128)(2...) while((s32[]{:T(128)}, ...), condition=%wide.region_4.5_spmd.clone, body=%wide.region_1.0_spmd.clone.sunk | while | flops 537869568 | bytes 19884240 | solution.py:71
  63.7 0.6 dynamic_slice.43
  64.8 0.1 broadcast_in_dim.83
  64.9 2.0 %fusion.35 = (f32[384]{0:T(512)S(1)}, f32[384,2688]{1,0:T(8,128)S(1)}) fusion(bf16[2688,256]{1,0:T(8,128)(2,1)} %get-tuple-element.179, s32[]{:T(128)S(6)} %select_n.38, bf16[384,256]{1,0:T(8,128)(2,1)S(1)} %get-tuple-element.178, pred[2688]{0:T(1024)(128)(4,1)S(1)} %broadcast_in_dim.84), kind=kOutput, calls=%fused_computation.39.clone.1 | convolution fusion | flops 267337344 | bytes 4920832 | tf_op jit(solution)/shard_map/while/body/eval_jaxpr/while/body/eval_jaxpr/qd,kd->qk/dot_general | solution.py:61
  66.9 0.0 copy-start.5
  66.9 0.9 fusion.36
  67.8 0.5 copy-done.5
  68.3 0.8 fusion.37
  69.0 0.1 copy.12
  69.2 0.6 dynamic_slice.43
  70.4 0.1 broadcast_in_dim.83
  70.4 2.0 %fusion.35 = (f32[384]{0:T(512)S(1)}, f32[384,2688]{1,0:T(8,128)S(1)}) fusion(bf16[2688,256]{1,0:T(8,128)(2,1)} %get-tuple-element.179, s32[]{:T(128)S(6)} %select_n.38, bf16[384,256]{1,0:T(8,128)(2,1)S(1)} %get-tuple-element.178, pred[2688]{0:T(1024)(128)(4,1)S(1)} %broadcast_in_dim.84), kind=kOutput, calls=%fused_computation.39.clone.1 | convolution fusion | flops 267337344 | bytes 4920832 | tf_op jit(solution)/shard_map/while/body/eval_jaxpr/while/body/eval_jaxpr/qd,kd->qk/dot_general | solution.py:61
  72.5 0.0 copy-start.5
  72.5 0.9 fusion.36
  73.3 0.5 copy-done.5
  73.8 0.8 fusion.37
  74.6 0.1 copy.12
  74.7 0.0 copy-done
  74.8 3.1 %convolution_convert_fusion = bf16[384,5120]{1,0:T(8,128)(2,1)} fusion(bf16[384,256]{0,1:T(8,128)(2,1)S(1)} %bitcast.15, bf16[256,5120]{1,0:T(8,128)(2,1)S(1)} %copy-done), kind=kOutput, calls=%fused_computation.20 | convolution fusion | flops 1008599040 | bytes 6750208 | tf_op jit(solution)/shard_map/dot_general | solution.py:78
  77.8 0.0 reduce-scatter.2.cloned.1.call-update
  77.9 47.4 %reduce-scatter.2.cloned.1.call-done = bf16[96,5120]{1,0:T(8,128)(2,1)} async-done(((bf16[384,5120]{1,0:T(8,128)(2,1)}), bf16[96,5120]{1,0:T(8,128)(2,1)}) %reduce-scatter.2.cloned.1.call-update) | async-done | bytes 983056 | tf_op jit(solution)/shard_map/reduce_scatter | solution.py:77
  (19 shorter events, 0.3 us)
Async XLA Ops:
  6.5 68.2 %copy-start = (bf16[256,5120]{1,0:T(8,128)(2,1)S(1)}, bf16[256,5120]{1,0:T(8,128)(2,1)}, u32[]{:S(2)}) copy-start(bf16[256,5120]{1,0:T(8,128)(2,1)} %param.11) | copy-start | bytes 7864324
  6.5 33.7 %copy-start.3 = (bf16[384,256]{1,0:T(8,128)(2,1)S(1)}, bf16[384,256]{1,0:T(8,128)(2,1)}, u32[]{:S(2)}) copy-start(bf16[384,256]{1,0:T(8,128)(2,1)} %param.10) | copy-start | bytes 589828
  6.5 118.7 %reduce-scatter.2.cloned.1.call-start = ((), (), s32[]{:S(2)}) async-start(), calls=%async_computation.1 | async-start | bytes 4915200 | tf_op jit(solution)/shard_map/reduce_scatter | solution.py:77
  6.5 17.9 %collective-permute-start = (bf16[384,256]{1,0:T(8,128)(2,1)}, bf16[384,256]{1,0:T(8,128)(2,1)}, u32[]{:S(2)}, u32[]{:S(2)}) collective-permute-start(bf16[384,256]{1,0:T(8,128)(2,1)} %param.9), channel_id=1, source_target_pairs={{0,12},{4,16},{8,20},{12,24},{16,28},{1,13},{5,17},{9,21},{13,25},... | collective-permute-start | bytes 589832 | tf_op jit(solution)/shard_map/ppermute | solution.py:15
  13.4 13.3 %collective-permute-start.1 = (bf16[384,256]{1,0:T(8,128)(2,1)}, bf16[384,256]{1,0:T(8,128)(2,1)}, u32[]{:S(2)}, u32[]{:S(2)}) collective-permute-start(bf16[384,256]{1,0:T(8,128)(2,1)} %param.9), channel_id=1, source_target_pairs={{0,8},{4,12},{8,16},{12,20},{16,24},{20,28},{1,9},{5,13},{9,17},{1... | collective-permute-start | bytes 589832 | tf_op jit(solution)/shard_map/ppermute | solution.py:15
  17.5 17.4 %collective-permute-start.2 = (bf16[384,256]{1,0:T(8,128)(2,1)}, bf16[384,256]{1,0:T(8,128)(2,1)S(1)}, u32[]{:S(2)}, u32[]{:S(2)}) collective-permute-start(bf16[384,256]{1,0:T(8,128)(2,1)} %param.9), channel_id=1, source_target_pairs={{0,4},{4,8},{8,12},{12,16},{16,20},{20,24},{24,28},{1,5},{5,9},{9,... | collective-permute-start | bytes 589832 | tf_op jit(solution)/shard_map/ppermute | solution.py:15
  20.3 30.5 %collective-permute-start.3 = (bf16[384,256]{1,0:T(8,128)(2,1)}, bf16[384,256]{1,0:T(8,128)(2,1)}, u32[]{:S(2)}, u32[]{:S(2)}) collective-permute-start(bf16[384,256]{1,0:T(8,128)(2,1)} %param.9), channel_id=1, source_target_pairs={{4,0},{8,4},{12,8},{16,12},{20,16},{24,20},{28,24},{5,1},{9,5},{13... | collective-permute-start | bytes 589832 | tf_op jit(solution)/shard_map/ppermute | solution.py:15
  21.6 31.6 %collective-permute-start.4 = (bf16[384,256]{1,0:T(8,128)(2,1)}, bf16[384,256]{1,0:T(8,128)(2,1)S(1)}, u32[]{:S(2)}, u32[]{:S(2)}) collective-permute-start(bf16[384,256]{1,0:T(8,128)(2,1)} %param.9), channel_id=1, source_target_pairs={{8,0},{12,4},{16,8},{20,12},{24,16},{28,20},{9,1},{13,5},{17,9},{2... | collective-permute-start | bytes 589832 | tf_op jit(solution)/shard_map/ppermute | solution.py:15
  24.4 28.8 %collective-permute-start.5 = (bf16[384,256]{1,0:T(8,128)(2,1)}, bf16[384,256]{1,0:T(8,128)(2,1)S(1)}, u32[]{:S(2)}, u32[]{:S(2)}) collective-permute-start(bf16[384,256]{1,0:T(8,128)(2,1)} %param.9), channel_id=1, source_target_pairs={{12,0},{16,4},{20,8},{24,12},{28,16},{13,1},{17,5},{21,9},{25,13},... | collective-permute-start | bytes 589832 | tf_op jit(solution)/shard_map/ppermute | solution.py:15
  26.7 13.6 %collective-permute-start.6 = (bf16[384,256]{1,0:T(8,128)(2,1)}, bf16[384,256]{1,0:T(8,128)(2,1)S(1)}, u32[]{:S(2)}, u32[]{:S(2)}) collective-permute-start(bf16[384,256]{1,0:T(8,128)(2,1)} %param.10), channel_id=1, source_target_pairs={{0,12},{4,16},{8,20},{12,24},{16,28},{1,13},{5,17},{9,21},{13,25},... | collective-permute-start | bytes 589832 | tf_op jit(solution)/shard_map/ppermute | solution.py:15
  34.9 9.2 %collective-permute-start.7 = (bf16[384,256]{1,0:T(8,128)(2,1)}, bf16[384,256]{1,0:T(8,128)(2,1)S(1)}, u32[]{:S(2)}, u32[]{:S(2)}) collective-permute-start(bf16[384,256]{1,0:T(8,128)(2,1)} %param.10), channel_id=1, source_target_pairs={{0,8},{4,12},{8,16},{12,20},{16,24},{20,28},{1,9},{5,13},{9,17},{1... | collective-permute-start | bytes 589832 | tf_op jit(solution)/shard_map/ppermute | solution.py:15
  40.3 9.2 %collective-permute-start.8 = (bf16[384,256]{1,0:T(8,128)(2,1)S(1)}, bf16[384,256]{1,0:T(8,128)(2,1)S(1)}, u32[]{:S(2)}, u32[]{:S(2)}) collective-permute-start(bf16[384,256]{1,0:T(8,128)(2,1)S(1)} %copy-done.3), channel_id=1, source_target_pairs={{0,4},{4,8},{8,12},{12,16},{16,20},{20,24},{24,28},{1,5},{5,9},{9,... | collective-permute-start | bytes 589832 | tf_op jit(solution)/shard_map/ppermute | solution.py:15
  44.2 9.1 %collective-permute-start.9 = (bf16[384,256]{1,0:T(8,128)(2,1)S(1)}, bf16[384,256]{1,0:T(8,128)(2,1)S(1)}, u32[]{:S(2)}, u32[]{:S(2)}) collective-permute-start(bf16[384,256]{1,0:T(8,128)(2,1)S(1)} %copy-done.3), channel_id=1, source_target_pairs={{4,0},{8,4},{12,8},{16,12},{20,16},{24,20},{28,24},{5,1},{9,5},{13... | collective-permute-start | bytes 589832 | tf_op jit(solution)/shard_map/ppermute | solution.py:15
  49.4 8.4 %collective-permute-start.10 = (bf16[384,256]{1,0:T(8,128)(2,1)S(1)}, bf16[384,256]{1,0:T(8,128)(2,1)S(1)}, u32[]{:S(2)}, u32[]{:S(2)}) collective-permute-start(bf16[384,256]{1,0:T(8,128)(2,1)S(1)} %copy-done.3), channel_id=1, source_target_pairs={{8,0},{12,4},{16,8},{20,12},{24,16},{28,20},{9,1},{13,5},{17,9},{2... | collective-permute-start | bytes 589832 | tf_op jit(solution)/shard_map/ppermute | solution.py:15
  50.7 12.9 %copy-start.2 = (bf16[384,256]{1,0:T(8,128)(2,1)S(1)}, bf16[384,256]{1,0:T(8,128)(2,1)}, u32[]{:S(2)}) copy-start(bf16[384,256]{1,0:T(8,128)(2,1)} %param.8) | copy-start | bytes 589828
  50.8 11.8 %collective-permute-start.11 = (bf16[384,256]{1,0:T(8,128)(2,1)S(1)}, bf16[384,256]{1,0:T(8,128)(2,1)S(1)}, u32[]{:S(2)}, u32[]{:S(2)}) collective-permute-start(bf16[384,256]{1,0:T(8,128)(2,1)S(1)} %copy-done.3), channel_id=1, source_target_pairs={{12,0},{16,4},{20,8},{24,12},{28,16},{13,1},{17,5},{21,9},{25,13},... | collective-permute-start | bytes 589832 | tf_op jit(solution)/shard_map/ppermute | solution.py:15
  53.2 9.3 %copy-start.1 = (bf16[2688,256]{1,0:T(8,128)(2,1)}, bf16[2688,256]{1,0:T(8,128)(2,1)S(1)}, u32[]{:S(2)}) copy-start(bf16[2688,256]{1,0:T(8,128)(2,1)S(1)} %constant_dynamic-update-slice_fusion.1) | copy-start | bytes 4128772
  62.6 1.1 copy-start.4
  66.9 1.3 %copy-start.5 = (bf16[2688,256]{1,0:T(8,128)(2,1)S(1)}, bf16[2688,256]{1,0:T(8,128)(2,1)}, u32[]{:S(2)}) copy-start(bf16[2688,256]{1,0:T(8,128)(2,1)} %get-tuple-element.180) | copy-start | bytes 4128772 | tf_op jit(solution)/shard_map/while/body/eval_jaxpr/while
  72.5 1.3 %copy-start.5 = (bf16[2688,256]{1,0:T(8,128)(2,1)S(1)}, bf16[2688,256]{1,0:T(8,128)(2,1)}, u32[]{:S(2)}) copy-start(bf16[2688,256]{1,0:T(8,128)(2,1)} %get-tuple-element.180) | copy-start | bytes 4128772 | tf_op jit(solution)/shard_map/while/body/eval_jaxpr/while
Sparse Core Ops, SparseCore 0:
  78.0 47.2 reduce-scatter.1
where the time goes:
time: 133 us; the launch traced here: 132 us
  waiting for transfers between devices  61.3 us (46%)
  starting transfers between devices  36.4 us (27%)
  between operations  14.3 us (11%)
  matrix products  8.63 us (6%)
  local copies, waits for them, and re-layouts  7.6 us (6%)
  other arithmetic  2.57 us (2%)
    reduce_scatter x1, waiting for transfers between devices, local(): lax.psum_scatter(jnp.dot(attended, out_weight, preferred_element_type=jnp...  47.4 us
    ppermute x12, starting transfers between devices, passed_along(): lax.ppermute(value, axis, [(source, source + steps) for source in range(f...  36.4 us
    ppermute x12, waiting for transfers between devices, passed_along(): lax.ppermute(value, axis, [(source, source + steps) for source in range(f...  13.9 us
    unnamed x22, local copies, waits for them, and re-layouts  4.96 us
    dot_general x2, matrix products, one_head(): jnp.einsum('qd,kd->qk', q_head, k_head, preferred_element_type=jnp.float32)  4.01 us
    dot_general x1, matrix products, local(): jnp.dot(attended, out_weight, preferred_element_type=jnp.float32)  3.09 us
  transfers between devices with their start and end apart: 13, of which 5 were waited for; matrix products, arithmetic and copies ran while one was open for 4% of the time, Pallas kernels for 0%

commit v1 on v0

v1 whole, which is shorter than its diff:
```python
import functools
import math

import jax
import jax.numpy as jnp
from jax import lax
from jax.experimental import pallas as pl
from jax.experimental.pallas import tpu as pltpu
from jax.sharding import PartitionSpec as P

HD = 128
REACH = 3
NEG = -1e30
GATHERED = 2560


def attend_kernel(tile_ref, list_ref, count_ref, q_ref, *refs):
    tiles, out_ref = refs[: 2 * REACH + 1], refs[2 * REACH + 1]
    max_ref, sum_ref, acc_ref = refs[2 * REACH + 2 :]
    rows, width = q_ref.shape
    heads = width // HD
    tile_index = tile_ref[0]
    max_ref[...] = jnp.full_like(max_ref, NEG)
    sum_ref[...] = jnp.zeros_like(sum_ref)
    acc_ref[...] = jnp.zeros_like(acc_ref)
    for offset in range(-REACH, REACH + 1):
        target = tile_index + offset
        listed = jnp.bool_(False)
        for slot in range(list_ref.shape[1]):
            listed |= (list_ref[0, slot] == target) & (slot < count_ref[0])
        tile = tiles[offset + REACH]

        @pl.when(listed & (target >= 0))
        def _():
            for head in range(heads):
                cols = slice(head * HD, (head + 1) * HD)
                k_head = tile[:, cols]
                v_head = tile[:, slice(width + head * HD, width + (head + 1) * HD)]
                scores = lax.dot_general(
                    q_ref[:, cols],
                    k_head,
                    (((1,), (1,)), ((), ())),
                    preferred_element_type=jnp.float32,
                ) * (1.0 / math.sqrt(HD))
                old = max_ref[:, head : head + 1]
                new = jnp.maximum(old, jnp.max(scores, axis=1, keepdims=True))
                weights = jnp.exp(scores - new)
                shrink = jnp.exp(old - new)
                sum_ref[:, head : head + 1] = sum_ref[:, head : head + 1] * shrink + jnp.sum(
                    weights, axis=1, keepdims=True
                )
                max_ref[:, head : head + 1] = new
                acc_ref[:, cols] = acc_ref[:, cols] * shrink + jnp.dot(
                    weights.astype(jnp.bfloat16), v_head, preferred_element_type=jnp.float32
                )

    for head in range(heads):
        cols = slice(head * HD, (head + 1) * HD)
        out_ref[:, cols] = (acc_ref[:, cols] / sum_ref[:, head : head + 1]).astype(out_ref.dtype)


def attend(tile_index, neighbours, counts, queries, tiles):
    rows, width = queries.shape
    heads = width // HD
    area = rows * rows * len(tiles) * heads
    smem = pl.BlockSpec(memory_space=pltpu.SMEM)
    vmem = pl.BlockSpec(memory_space=pltpu.VMEM)
    return pl.pallas_call(
        attend_kernel,
        out_shape=jax.ShapeDtypeStruct((rows, width), jnp.bfloat16),
        in_specs=[smem] * 3 + [vmem] * (1 + len(tiles)),
        out_specs=vmem,
        scratch_shapes=[
            pltpu.VMEM((rows, heads), jnp.float32),
            pltpu.VMEM((rows, heads), jnp.float32),
            pltpu.VMEM((rows, width), jnp.float32),
        ],
        compiler_params=pltpu.CompilerParams(vmem_limit_bytes=32 * 1024 * 1024),
        cost_estimate=pl.CostEstimate(
            flops=4 * area * HD,
            bytes_accessed=2 * rows * width * (2 + 2 * len(tiles)),
            transcendentals=area,
        ),
    )(tile_index, neighbours, counts, queries, *tiles)


def shifted(value, axis, steps):
    count = lax.axis_size(axis)
    first, last = (max(0, -steps), min(count, count - steps))
    return lax.ppermute(value, axis, [(source, source + steps) for source in range(first, last)])


def swap_cores(value):
    count = lax.axis_size("head")
    return lax.ppermute(value, "head", [(i, i ^ 1) for i in range(count)])


def from_chip(value, steps):
    count = lax.axis_size("head")
    return lax.ppermute(value, "head", [((i + 2 * steps) % count, i) for i in range(count)])


def local(queries, keys, values, out_weight, neighbours, counts):
    rows, width = queries.shape
    n_head = lax.axis_size("head")
    chips = n_head // 2
    own_rows = rows // n_head
    head_index = lax.axis_index("head")
    chip, core = head_index // 2, head_index % 2
    model = out_weight.shape[1]
    gathered = GATHERED if chips == 2 else 0
    f32 = jnp.float32

    both = jnp.concatenate([keys, values], axis=1)
    tiles = {0: both}
    for distance in range(REACH, 0, -1):
        tiles[-distance] = shifted(both, "ctx", distance)
        tiles[distance] = shifted(both, "ctx", -distance)

    weight_pair = swap_cores(out_weight)
    far = []
    for steps in range(1, chips):
        if gathered:
            other = from_chip(out_weight[:, :gathered], steps)
            far.append((other, swap_cores(other)))

    tile_index = lax.axis_index("ctx").astype(jnp.int32).reshape(1)
    attended = attend(
        tile_index,
        neighbours,
        counts,
        queries,
        [tiles[offset] for offset in range(-REACH, REACH + 1)],
    )

    blocks = attended.reshape(chips, 2, own_rows, width)
    mine = lax.dynamic_index_in_dim(blocks, core, 1, keepdims=False)
    theirs = lax.dynamic_index_in_dim(blocks, 1 - core, 1, keepdims=False)
    joined = jnp.concatenate([mine, swap_cores(theirs)], axis=2)

    def project(block, weights):
        return jnp.dot(block[:, :width], weights[0], preferred_element_type=f32) + jnp.dot(
            block[:, width:], weights[1], preferred_element_type=f32
        )

    near = (out_weight, weight_pair)
    right = [weight[:, gathered:] for weight in near]
    received, received_blocks = [], []
    for steps in range(1, chips):
        block = lax.dynamic_index_in_dim(joined, (chip - steps) % chips, 0, keepdims=False)
        received.append(from_chip(project(block, right).astype(jnp.bfloat16), steps))
        if gathered:
            received_blocks.append(from_chip(block, steps))
    own = lax.dynamic_index_in_dim(joined, chip, 0, keepdims=False)
    total = project(own, right)
    for partial in received:
        total = total + partial.astype(f32)
    total = total.astype(jnp.bfloat16)
    if gathered:
        left = project(own, [weight[:, :gathered] for weight in near])
        for block, weights in zip(received_blocks, far):
            left = left + project(block, weights)
        total = jnp.concatenate([left.astype(jnp.bfloat16), total], axis=1)
    return total


def solution(mesh):
    placed = (
        P("ctx", "head"),
        P("ctx", "head"),
        P("ctx", "head"),
        P("head", None),
        P("ctx", None),
        P("ctx"),
    )
    return jax.shard_map(
        local, mesh=mesh, in_specs=placed, out_specs=P(("ctx", "head"), None), check_vma=False
    )
```

time: 133 us -> 98.9 us (0.74)
  the two profiles are of different devices: /device:TPU:0 before, /device:TPU:16 now
where the time goes in v1:
time: 98.9 us; the launch traced here: 98.4 us
  waiting for transfers between devices  44.8 us (45%)
  starting transfers between devices  26.5 us (27%)
  Pallas kernels  11.4 us (12%)
  matrix products  9.37 us (9%)
  local copies, waits for them, and re-layouts  4.39 us (4%)
  other arithmetic  1.04 us (1%)
    ppermute x6, waiting for transfers between devices, shifted(): lax.ppermute(value, axis, [(source, source + steps) for source in range(f...  33.4 us
    ppermute x6, starting transfers between devices, shifted(): lax.ppermute(value, axis, [(source, source + steps) for source in range(f...  21.8 us
    pallas_call x1, Pallas kernels, attend(): pl.pallas_call(attend_kernel, out_shape=jax.ShapeDtypeStruct((rows, width...  11.4 us
    ppermute x3, waiting for transfers between devices, from_chip(): lax.ppermute(value, 'head', [((i + 2 * steps) % count, i) for i in range(...  10.1 us
    dot_general x4, matrix products, project(): jnp.dot(block[:, width:], weights[1], preferred_element_type=f32)  5.35 us
    ppermute x3, starting transfers between devices, from_chip(): lax.ppermute(value, 'head', [((i + 2 * steps) % count, i) for i in range(...  4.6 us
    dot_general x4, matrix products, project(): jnp.dot(block[:, :width], weights[0], preferred_element_type=f32)  4.03 us
    slice x1, local copies, waits for them, and re-layouts, local(): left = project(own, [weight[:, :gathered] for weight in near])  2.47 us
  transfers between devices with their start and end apart: 12, of which 7 were waited for; matrix products, arithmetic and copies ran while one was open for 12% of the time, Pallas kernels for 12%

profile of v1, /device:TPU:16, one launch (start us, length us, event | category | flops | bytes accessed | tf_op | source)
XLA Modules:
  0.0 98.4 jit_solution(16251392926389435834)
XLA Ops:
  0.0 0.0 collective-permute-start.7
  0.0 0.9 constant_dynamic-update-slice_fusion.1
  0.9 0.9 constant_dynamic-update-slice_fusion.refs_3_
  1.9 0.0 copy-start
  1.9 0.0 copy-start.1
  1.9 4.6 %collective-permute-start = (bf16[384,512]{1,0:T(8,128)(2,1)S(1)}, bf16[384,512]{1,0:T(8,128)(2,1)S(1)}, u32[]{:S(2)}, u32[]{:S(2)}) collective-permute-start(bf16[384,512]{1,0:T(8,128)(2,1)S(1)} %constant_dynamic-update-slice_fusion.refs_3_), channel_id=1, source_target_pairs={{0,12},{4,16},{8,20},{12,24},{16,28},{1,13},{5,17},{9,21},{13,25},... | collective-permute-start | bytes 1179656 | tf_op jit(solution)/shard_map/ppermute | solution.py:90
  6.5 1.9 %collective-permute-start.1 = (bf16[384,512]{1,0:T(8,128)(2,1)S(1)}, bf16[384,512]{1,0:T(8,128)(2,1)S(1)}, u32[]{:S(2)}, u32[]{:S(2)}) collective-permute-start(bf16[384,512]{1,0:T(8,128)(2,1)S(1)} %constant_dynamic-update-slice_fusion.refs_3_), channel_id=1, source_target_pairs={{0,8},{4,12},{8,16},{12,20},{16,24},{20,28},{1,9},{5,13},{9,17},{1... | collective-permute-start | bytes 1179656 | tf_op jit(solution)/shard_map/ppermute | solution.py:90
  8.4 1.9 %collective-permute-start.2 = (bf16[384,512]{1,0:T(8,128)(2,1)S(1)}, bf16[384,512]{1,0:T(8,128)(2,1)S(1)}, u32[]{:S(2)}, u32[]{:S(2)}) collective-permute-start(bf16[384,512]{1,0:T(8,128)(2,1)S(1)} %constant_dynamic-update-slice_fusion.refs_3_), channel_id=1, source_target_pairs={{0,4},{4,8},{8,12},{12,16},{16,20},{20,24},{24,28},{1,5},{5,9},{9,... | collective-permute-start | bytes 1179656 | tf_op jit(solution)/shard_map/ppermute | solution.py:90
  10.4 2.5 %slice.34 = bf16[256,2560]{1,0:T(8,128)(2,1)} slice(bf16[256,5120]{1,0:T(8,128)(2,1)} %param.9), slice={[0:256], [0:2560]} | slice | bytes 2621440 | tf_op jit(solution)/shard_map/slice | solution.py:160
  12.8 1.5 %collective-permute-start.9 = (bf16[256,2560]{1,0:T(8,128)(2,1)}, bf16[256,2560]{1,0:T(8,128)(2,1)}, u32[]{:S(2)}, u32[]{:S(2)}) collective-permute-start(bf16[256,2560]{1,0:T(8,128)(2,1)} %slice.34), channel_id=1, source_target_pairs={{2,0},{3,1},{0,2},{1,3},{6,4},{7,5},{4,6},{5,7},{10,8},{11,9},{8,1... | collective-permute-start | bytes 3932168 | tf_op jit(solution)/shard_map/ppermute | solution.py:100
  14.3 3.4 %collective-permute-done.refs_0_ = bf16[384,512]{1,0:T(8,128)(2,1)S(1)} collective-permute-done((bf16[384,512]{1,0:T(8,128)(2,1)S(1)}, bf16[384,512]{1,0:T(8,128)(2,1)S(1)}, u32[]{:S(2)}, u32[]{:S(2)}) %collective-permute-start) | collective-permute-done | bytes 393248 | tf_op jit(solution)/shard_map/ppermute | solution.py:90
  17.7 9.5 %collective-permute-start.3 = (bf16[384,512]{1,0:T(8,128)(2,1)S(1)}, bf16[384,512]{1,0:T(8,128)(2,1)S(1)}, u32[]{:S(2)}, u32[]{:S(2)}) collective-permute-start(bf16[384,512]{1,0:T(8,128)(2,1)S(1)} %constant_dynamic-update-slice_fusion.refs_3_), channel_id=1, source_target_pairs={{4,0},{8,4},{12,8},{16,12},{20,16},{24,20},{28,24},{5,1},{9,5},{13... | collective-permute-start | bytes 1179656 | tf_op jit(solution)/shard_map/ppermute | solution.py:90
  27.2 0.0 collective-permute-done.1.refs_1_
  27.2 1.9 %collective-permute-start.4 = (bf16[384,512]{1,0:T(8,128)(2,1)S(1)}, bf16[384,512]{1,0:T(8,128)(2,1)S(1)}, u32[]{:S(2)}, u32[]{:S(2)}) collective-permute-start(bf16[384,512]{1,0:T(8,128)(2,1)S(1)} %constant_dynamic-update-slice_fusion.refs_3_), channel_id=1, source_target_pairs={{8,0},{12,4},{16,8},{20,12},{24,16},{28,20},{9,1},{13,5},{17,9},{2... | collective-permute-start | bytes 1179656 | tf_op jit(solution)/shard_map/ppermute | solution.py:90
  29.2 13.4 %collective-permute-done.2.refs_2_ = bf16[384,512]{1,0:T(8,128)(2,1)S(1)} collective-permute-done((bf16[384,512]{1,0:T(8,128)(2,1)S(1)}, bf16[384,512]{1,0:T(8,128)(2,1)S(1)}, u32[]{:S(2)}, u32[]{:S(2)}) %collective-permute-start.2) | collective-permute-done | bytes 393248 | tf_op jit(solution)/shard_map/ppermute | solution.py:90
  42.6 1.9 %collective-permute-start.5 = (bf16[384,512]{1,0:T(8,128)(2,1)S(1)}, bf16[384,512]{1,0:T(8,128)(2,1)S(1)}, u32[]{:S(2)}, u32[]{:S(2)}) collective-permute-start(bf16[384,512]{1,0:T(8,128)(2,1)S(1)} %constant_dynamic-update-slice_fusion.refs_3_), channel_id=1, source_target_pairs={{12,0},{16,4},{20,8},{24,12},{28,16},{13,1},{17,5},{21,9},{25,13},... | collective-permute-start | bytes 1179656 | tf_op jit(solution)/shard_map/ppermute | solution.py:90
  45.2 0.0 collective-permute-done.3.refs_4_
  45.2 2.3 %collective-permute-done.4.refs_5_ = bf16[384,512]{1,0:T(8,128)(2,1)S(1)} collective-permute-done((bf16[384,512]{1,0:T(8,128)(2,1)S(1)}, bf16[384,512]{1,0:T(8,128)(2,1)S(1)}, u32[]{:S(2)}, u32[]{:S(2)}) %collective-permute-start.4) | collective-permute-done | bytes 393248 | tf_op jit(solution)/shard_map/ppermute | solution.py:90
  47.5 14.3 %collective-permute-done.5.refs_6_ = bf16[384,512]{1,0:T(8,128)(2,1)S(1)} collective-permute-done((bf16[384,512]{1,0:T(8,128)(2,1)S(1)}, bf16[384,512]{1,0:T(8,128)(2,1)S(1)}, u32[]{:S(2)}, u32[]{:S(2)}) %collective-permute-start.5) | collective-permute-done | bytes 393248 | tf_op jit(solution)/shard_map/ppermute | solution.py:90
  61.8 0.0 copy-done
  61.8 0.0 copy-done.1
  61.8 11.4 %shard_map.64 = bf16[384,256]{1,0:T(8,128)(2,1)S(1)} custom-call(s32[1]{0:T(128)} %bitcast.tile_ref, s32[1,7]{1,0:T(1,128)S(1)} %copy-done.1, s32[1]{0:T(128)S(6)} %copy.8.count_ref, bf16[384,256]{1,0:T(8,128)(2,1)S(1)} %copy-done, bf16[384,512]{1,0:T(8,128)(2,1)S(1)} %collective-permute-done.refs_0_, bf16[384,512]{1,0:T(8,128)(2,1)S(1)} %collective-permute-done.1.refs_1_, ...), custom_call_target="tpu_custom_call" | custom-call | flops 1056964608 | bytes 3145728 | tf_op jit(solution)/shard_map/pallas_call | solution.py:68
  73.3 0.1 collective-permute-start.6
  73.4 1.2 %collective-permute-done.6 = bf16[2,96,256]{2,1,0:T(8,128)(2,1)S(1)} collective-permute-done((bf16[2,96,256]{2,1,0:T(8,128)(2,1)S(1)}, bf16[2,96,256]{2,1,0:T(8,128)(2,1)S(1)}, u32[]{:S(2)}, u32[]{:S(2)}) %collective-permute-start.6) | collective-permute-done | bytes 98336 | tf_op jit(solution)/shard_map/ppermute | solution.py:95
  74.6 0.0 copy-start.2
  74.7 1.6 %collective-permute-start.8 = (bf16[96,512]{1,0:T(8,128)(2,1)S(1)}, bf16[96,512]{1,0:T(8,128)(2,1)S(1)}, u32[]{:S(2)}, u32[]{:S(2)}) collective-permute-start(bf16[96,512]{1,0:T(8,128)(2,1)S(1)} %get-tuple-element.5), channel_id=1, source_target_pairs={{2,0},{3,1},{0,2},{1,3},{6,4},{7,5},{4,6},{5,7},{10,8},{11,9},{8,1... | collective-permute-start | bytes 294920 | tf_op jit(solution)/shard_map/ppermute | solution.py:100
  76.2 1.7 %fusion.8 = f32[96,2560]{1,0:T(8,128)S(1)} fusion(bf16[256,5120]{1,0:T(8,128)(2,1)} %param.9, bf16[96,512]{1,0:T(8,128)(2,1)S(1)} %get-tuple-element.5), kind=kOutput, calls=%fused_computation.12 | convolution fusion | flops 125829120 | bytes 2342912 | tf_op jit(solution)/shard_map/dot_general | solution.py:142
  77.9 0.0 collective-permute-done.9
  77.9 0.1 collective-permute-start.10
  78.0 0.0 copy-done.2
  78.0 0.3 fusion.10
  78.3 0.4 fusion.24
  78.7 0.9 collective-permute-done.8
  79.6 1.7 %fusion.19 = f32[96,2560]{1,0:T(8,128)S(1)} fusion(bf16[256,2560]{1,0:T(8,128)(2,1)} %collective-permute-done.9, bf16[96,512]{1,0:T(8,128)(2,1)S(1)} %collective-permute-done.8), kind=kOutput, calls=%fused_computation.30 | convolution fusion | flops 125829120 | bytes 2342912 | tf_op jit(solution)/shard_map/dot_general | solution.py:142
  81.2 0.0 collective-permute-done.7
  81.2 1.7 %fusion.4 = bf16[96,2560]{1,0:T(8,128)(2,1)S(1)} fusion(f32[96,2560]{1,0:T(8,128)S(1)} %fusion.8, bf16[256,5120]{1,0:T(8,128)(2,1)} %collective-permute-done.7, bf16[96,512]{1,0:T(8,128)(2,1)S(1)} %get-tuple-element.5), kind=kOutput, calls=%fused_computation.8 | convolution fusion | flops 126320640 | bytes 2834432 | tf_op jit(solution)/shard_map/dot_general | solution.py:142
  82.9 1.6 %collective-permute-start.11 = (bf16[96,2560]{1,0:T(8,128)(2,1)S(1)}, bf16[96,2560]{1,0:T(8,128)(2,1)S(1)}, u32[]{:S(2)}, u32[]{:S(2)}) collective-permute-start(bf16[96,2560]{1,0:T(8,128)(2,1)S(1)} %fusion.4), channel_id=1, source_target_pairs={{2,0},{3,1},{0,2},{1,3},{6,4},{7,5},{4,6},{5,7},{10,8},{11,9},{8,1... | collective-permute-start | bytes 1474568 | tf_op jit(solution)/shard_map/ppermute | solution.py:100
  84.5 1.7 %convolution_add_fusion.3 = f32[96,2560]{1,0:T(8,128)S(1)} fusion(f32[96,2560]{1,0:T(8,128)S(1)} %fusion.24, bf16[256,5120]{1,0:T(8,128)(2,1)} %collective-permute-done.7, bf16[96,512]{1,0:T(8,128)(2,1)S(1)} %get-tuple-element.6), kind=kOutput, calls=%fused_computation.5 | convolution fusion | flops 126074880 | bytes 3325952 | tf_op jit(solution)/shard_map/dot_general | solution.py:142
  86.1 0.0 collective-permute-done.10
  86.1 0.4 fusion.2
  86.5 9.2 %collective-permute-done.11 = bf16[96,2560]{1,0:T(8,128)(2,1)S(1)} collective-permute-done((bf16[96,2560]{1,0:T(8,128)(2,1)S(1)}, bf16[96,2560]{1,0:T(8,128)(2,1)S(1)}, u32[]{:S(2)}, u32[]{:S(2)}) %collective-permute-start.11) | collective-permute-done | bytes 491552 | tf_op jit(solution)/shard_map/ppermute | solution.py:100
  95.7 1.7 %fusion.3 = bf16[96,2560]{1,0:T(8,128)(2,1)S(1)} fusion(f32[96,2560]{1,0:T(8,128)S(1)} %fusion.10, bf16[256,5120]{1,0:T(8,128)(2,1)} %collective-permute-done.7, bf16[96,2560]{1,0:T(8,128)(2,1)S(1)} %collective-permute-done.11, bf16[96,512]{1,0:T(8,128)(2,1)S(1)} %get-tuple-element.6), kind=kOutput, calls=%fused_computation.7 | convolution fusion | flops 126812160 | bytes 3325952 | tf_op jit(solution)/shard_map/dot_general | solution.py:142
  97.4 1.0 %pad_maximum_fusion = bf16[96,5120]{1,0:T(8,128)(2,1)} fusion(bf16[96,2560]{1,0:T(8,128)(2,1)S(1)} %fusion.3, bf16[96,2560]{1,0:T(8,128)(2,1)S(1)} %fusion.2), kind=kLoop, calls=%fused_computation.16 | loop fusion | flops 1966080 | bytes 1966080 | tf_op jit(solution)/shard_map/concatenate | solution.py:163
  (2 shorter events, 0.0 us)
Async XLA Ops:
  0.0 81.2 %collective-permute-start.7 = (bf16[256,5120]{1,0:T(8,128)(2,1)}, bf16[256,5120]{1,0:T(8,128)(2,1)}, u32[]{:S(2)}, u32[]{:S(2)}) collective-permute-start(bf16[256,5120]{1,0:T(8,128)(2,1)} %param.9), channel_id=1, source_target_pairs={{0,1},{1,0},{2,3},{3,2},{4,5},{5,4},{6,7},{7,6},{8,9},{9,8},{10,11... | collective-permute-start | bytes 7864328 | tf_op jit(solution)/shard_map/ppermute | solution.py:95
  1.9 59.9 %copy-start = (bf16[384,256]{1,0:T(8,128)(2,1)S(1)}, bf16[384,256]{1,0:T(8,128)(2,1)}, u32[]{:S(2)}) copy-start(bf16[384,256]{1,0:T(8,128)(2,1)} %q_ref.1) | copy-start | bytes 589828
  1.9 59.9 %copy-start.1 = (s32[1,7]{1,0:T(1,128)S(1)}, s32[1,7]{1,0:T(1,128)}, u32[]{:S(2)}) copy-start(s32[1,7]{1,0:T(1,128)} %list_ref.1) | copy-start | bytes 88
  1.9 15.8 %collective-permute-start = (bf16[384,512]{1,0:T(8,128)(2,1)S(1)}, bf16[384,512]{1,0:T(8,128)(2,1)S(1)}, u32[]{:S(2)}, u32[]{:S(2)}) collective-permute-start(bf16[384,512]{1,0:T(8,128)(2,1)S(1)} %constant_dynamic-update-slice_fusion.refs_3_), channel_id=1, source_target_pairs={{0,12},{4,16},{8,20},{12,24},{16,28},{1,13},{5,17},{9,21},{13,25},... | collective-permute-start | bytes 1179656 | tf_op jit(solution)/shard_map/ppermute | solution.py:90
  6.5 20.7 %collective-permute-start.1 = (bf16[384,512]{1,0:T(8,128)(2,1)S(1)}, bf16[384,512]{1,0:T(8,128)(2,1)S(1)}, u32[]{:S(2)}, u32[]{:S(2)}) collective-permute-start(bf16[384,512]{1,0:T(8,128)(2,1)S(1)} %constant_dynamic-update-slice_fusion.refs_3_), channel_id=1, source_target_pairs={{0,8},{4,12},{8,16},{12,20},{16,24},{20,28},{1,9},{5,13},{9,17},{1... | collective-permute-start | bytes 1179656 | tf_op jit(solution)/shard_map/ppermute | solution.py:90
  8.4 34.2 %collective-permute-start.2 = (bf16[384,512]{1,0:T(8,128)(2,1)S(1)}, bf16[384,512]{1,0:T(8,128)(2,1)S(1)}, u32[]{:S(2)}, u32[]{:S(2)}) collective-permute-start(bf16[384,512]{1,0:T(8,128)(2,1)S(1)} %constant_dynamic-update-slice_fusion.refs_3_), channel_id=1, source_target_pairs={{0,4},{4,8},{8,12},{12,16},{16,20},{20,24},{24,28},{1,5},{5,9},{9,... | collective-permute-start | bytes 1179656 | tf_op jit(solution)/shard_map/ppermute | solution.py:90
  12.8 65.1 %collective-permute-start.9 = (bf16[256,2560]{1,0:T(8,128)(2,1)}, bf16[256,2560]{1,0:T(8,128)(2,1)}, u32[]{:S(2)}, u32[]{:S(2)}) collective-permute-start(bf16[256,2560]{1,0:T(8,128)(2,1)} %slice.34), channel_id=1, source_target_pairs={{2,0},{3,1},{0,2},{1,3},{6,4},{7,5},{4,6},{5,7},{10,8},{11,9},{8,1... | collective-permute-start | bytes 3932168 | tf_op jit(solution)/shard_map/ppermute | solution.py:100
  17.7 27.5 %collective-permute-start.3 = (bf16[384,512]{1,0:T(8,128)(2,1)S(1)}, bf16[384,512]{1,0:T(8,128)(2,1)S(1)}, u32[]{:S(2)}, u32[]{:S(2)}) collective-permute-start(bf16[384,512]{1,0:T(8,128)(2,1)S(1)} %constant_dynamic-update-slice_fusion.refs_3_), channel_id=1, source_target_pairs={{4,0},{8,4},{12,8},{16,12},{20,16},{24,20},{28,24},{5,1},{9,5},{13... | collective-permute-start | bytes 1179656 | tf_op jit(solution)/shard_map/ppermute | solution.py:90
  27.2 20.3 %collective-permute-start.4 = (bf16[384,512]{1,0:T(8,128)(2,1)S(1)}, bf16[384,512]{1,0:T(8,128)(2,1)S(1)}, u32[]{:S(2)}, u32[]{:S(2)}) collective-permute-start(bf16[384,512]{1,0:T(8,128)(2,1)S(1)} %constant_dynamic-update-slice_fusion.refs_3_), channel_id=1, source_target_pairs={{8,0},{12,4},{16,8},{20,12},{24,16},{28,20},{9,1},{13,5},{17,9},{2... | collective-permute-start | bytes 1179656 | tf_op jit(solution)/shard_map/ppermute | solution.py:90
  42.6 19.2 %collective-permute-start.5 = (bf16[384,512]{1,0:T(8,128)(2,1)S(1)}, bf16[384,512]{1,0:T(8,128)(2,1)S(1)}, u32[]{:S(2)}, u32[]{:S(2)}) collective-permute-start(bf16[384,512]{1,0:T(8,128)(2,1)S(1)} %constant_dynamic-update-slice_fusion.refs_3_), channel_id=1, source_target_pairs={{12,0},{16,4},{20,8},{24,12},{28,16},{13,1},{17,5},{21,9},{25,13},... | collective-permute-start | bytes 1179656 | tf_op jit(solution)/shard_map/ppermute | solution.py:90
  73.3 1.4 %collective-permute-start.6 = (bf16[2,96,256]{2,1,0:T(8,128)(2,1)S(1)}, bf16[2,96,256]{2,1,0:T(8,128)(2,1)S(1)}, u32[]{:S(2)}, u32[]{:S(2)}) collective-permute-start(bf16[2,96,256]{2,1,0:T(8,128)(2,1)S(1)} %get-tuple-element.7), channel_id=1, source_target_pairs={{0,1},{1,0},{2,3},{3,2},{4,5},{5,4},{6,7},{7,6},{8,9},{9,8},{10,11... | collective-permute-start | bytes 294920 | tf_op jit(solution)/shard_map/ppermute | solution.py:95
  74.6 3.3 %copy-start.2 = (bf16[256,5120]{1,0:T(8,128)(2,1)S(1)}, bf16[256,5120]{1,0:T(8,128)(2,1)}, u32[]{:S(2)}) copy-start(bf16[256,5120]{1,0:T(8,128)(2,1)} %param.9) | copy-start | bytes 7864324
  74.7 4.9 %collective-permute-start.8 = (bf16[96,512]{1,0:T(8,128)(2,1)S(1)}, bf16[96,512]{1,0:T(8,128)(2,1)S(1)}, u32[]{:S(2)}, u32[]{:S(2)}) collective-permute-start(bf16[96,512]{1,0:T(8,128)(2,1)S(1)} %get-tuple-element.5), channel_id=1, source_target_pairs={{2,0},{3,1},{0,2},{1,3},{6,4},{7,5},{4,6},{5,7},{10,8},{11,9},{8,1... | collective-permute-start | bytes 294920 | tf_op jit(solution)/shard_map/ppermute | solution.py:100
  77.9 8.2 %collective-permute-start.10 = (bf16[256,2560]{1,0:T(8,128)(2,1)}, bf16[256,2560]{1,0:T(8,128)(2,1)S(1)}, u32[]{:S(2)}, u32[]{:S(2)}) collective-permute-start(bf16[256,2560]{1,0:T(8,128)(2,1)} %collective-permute-done.9), channel_id=1, source_target_pairs={{0,1},{1,0},{2,3},{3,2},{4,5},{5,4},{6,7},{7,6},{8,9},{9,8},{10,11... | collective-permute-start | bytes 3932168 | tf_op jit(solution)/shard_map/ppermute | solution.py:95
  82.9 12.8 %collective-permute-start.11 = (bf16[96,2560]{1,0:T(8,128)(2,1)S(1)}, bf16[96,2560]{1,0:T(8,128)(2,1)S(1)}, u32[]{:S(2)}, u32[]{:S(2)}) collective-permute-start(bf16[96,2560]{1,0:T(8,128)(2,1)S(1)} %fusion.4), channel_id=1, source_target_pairs={{2,0},{3,1},{0,2},{1,3},{6,4},{7,5},{4,6},{5,7},{10,8},{11,9},{8,1... | collective-permute-start | bytes 1474568 | tf_op jit(solution)/shard_map/ppermute | solution.py:100
